TPU v7x, 512 devices: a whole 4x8x8 slice. The times are simulated.
512 devices in a mesh: dp: 32 (over x, y), tp: 16 (over z, core).
Axes of the slice: x: 4, y: 8, z: 8, core: 2. Of those that a mesh axis runs over, the one named last changes fastest.
Arguments:
- embeddings: bfloat16 [12288, 192, 256], P(('dp', 'tp')), may hold values from -6 to 6
- projection: bfloat16 [256, 16], replicated, may hold values from -0.375 to 0.375
- compress: bfloat16 [256, 4], replicated, may hold values from -0.375 to 0.375
- w_up: bfloat16 [4096, 4096], P(None, 'tp'), may hold values from -0.09375 to 0.09375
- w_down: bfloat16 [4096, 768], P('tp'), may hold values from -0.125 to 0.125
- output_norm_gain: float32 [1536], P('tp'), may hold values from 0.25 to 1.75
- out_grad: bfloat16 [12288, 1536], P('dp', 'tp'), may hold values from -6 to 6
Outputs:
- block_result: bfloat16 [12288, 1536], P('dp', 'tp')
- grad_down: float32 [4096, 768], P(('tp', 'dp'))
All inputs are finite; a program needn't handle non-finite values.
Results may differ from a plain program's by a relative error of at most 0.017.
Values may be sent and summed in bfloat16 or wider, within the bound.
No kernel may reach another device: no remote copies, remote signals or barrier semaphores. Data moves between devices by JAX's collectives and lax.ppermute only.
A program may use at most 64 MiB of HBM per device.

v0:
```python
import jax
import jax.numpy as jnp
from jax import lax
from jax.sharding import PartitionSpec as P


def split_up(x, dim, devices):
    before, after = (x.shape[:dim], x.shape[dim + 1 :])
    return jnp.moveaxis(x.reshape(*before, devices, -1, *after), dim, 0)


def summed_on_arrival(x, axis, dim):
    parts = split_up(x, dim, lax.axis_size(axis))
    arrived = lax.all_to_all(parts, axis, split_axis=0, concat_axis=0, tiled=True)
    return arrived.astype(jnp.float32).sum(axis=0)


def sent_to_all(x, axis):
    devices = lax.axis_size(axis)
    return lax.all_to_all(jnp.broadcast_to(x[None], (devices, *x.shape)), axis, 0, 0, tiled=True)


def gathered_once(x, axis):
    leaves = jax.tree.leaves(x)
    sequence = sorted(range(len(leaves)), key=lambda k: -leaves[k].size)
    width = (1, *leaves[sequence[0]].shape)[-1]
    lines = [
        jnp.pad(leaves[k].reshape(-1), (0, -leaves[k].size % width)).reshape(-1, width)
        for k in sequence
    ]
    both, at, found = (sent_to_all(jnp.concatenate(lines), axis), 0, {})
    for k, line in zip(sequence, lines):
        share = both[:, at : at + len(line)].reshape(len(both), -1)
        found[k] = share[:, : leaves[k].size].reshape(-1, *leaves[k].shape)
        at += len(line)
    numbers = iter(range(len(leaves)))
    return jax.tree.map(lambda _: found[next(numbers)], x)


def joined_by_halves(pieces, combine):
    while len(jax.tree.leaves(pieces)[0]) > 1:
        pieces = jax.vmap(combine)(
            *(jax.tree.map(lambda part: part[side::2], pieces) for side in (0, 1))
        )
    return jax.tree.map(lambda part: part[0], pieces)


def joined_all(x, axis, combine):
    pieces = gathered_once(x, axis)
    return joined_by_halves(pieces, combine)


def turned_gather(arrays, axis, dims):
    turned = [jnp.moveaxis(a, dim, 0) for a, dim in zip(arrays, dims)]
    both = jnp.concatenate([t.reshape(len(t), -1) for t in turned], axis=1)
    filled, at, done = (lax.all_gather(both, axis, axis=0, tiled=True), 0, [])
    for t, dim in zip(turned, dims):
        share = filled[:, at : at + t[0].size].reshape(-1, *t.shape[1:])
        done.append(jnp.moveaxis(share, 0, dim))
        at += t[0].size
    return tuple(done)


def chan_merge(left, right):
    count_a, mean_a, dev_a = left
    count_b, mean_b, dev_b = right
    total = count_a + count_b
    delta = mean_b - mean_a
    row_average = mean_a + delta * (count_b / total)
    dev = dev_a + dev_b + delta * delta * (count_a * count_b / total)
    return (total, row_average, dev)


def on_device(embeddings, projection, compress, w_up, w_down, output_norm_gain, out_grad):
    samples = embeddings.shape[0]
    pairs = jnp.einsum(
        "sef,fk->sek", embeddings, projection, preferred_element_type=jnp.float32
    ).astype(jnp.bfloat16)
    inter = jnp.einsum(
        "sek,sef->skf", pairs, embeddings, preferred_element_type=jnp.float32
    ).reshape(samples, -1)
    center = inter - jnp.mean(inter, axis=1, keepdims=True)
    spread = jnp.mean(center * center, axis=1, keepdims=True)
    normed = (center / jnp.sqrt(spread + 1e-05)).astype(jnp.bfloat16)
    lcb = jnp.einsum(
        "sef,fj->sje", embeddings, compress, preferred_element_type=jnp.float32
    ).reshape(samples, -1)
    hidden = jax.nn.gelu(
        jnp.dot(
            lax.all_gather(normed, "tp", axis=0, tiled=True),
            w_up,
            preferred_element_type=jnp.float32,
        ),
        approximate=True,
    ).astype(jnp.bfloat16)
    group_rows = hidden.shape[0]
    tp_count = lax.axis_size("tp")
    mlp = jnp.dot(hidden, w_down, preferred_element_type=jnp.float32)
    mlp_width = mlp.shape[1]
    full_width = mlp_width + lcb.shape[1]
    width = full_width // tp_count
    mlp_share = summed_on_arrival(mlp.astype(jnp.bfloat16), "tp", 1)
    lcb_share = lax.all_to_all(
        lcb.astype(jnp.bfloat16), "tp", split_axis=1, concat_axis=0, tiled=True
    ).astype(lcb.dtype)
    mixed_rows = jnp.concatenate([mlp_share, lcb_share], axis=1)
    own_mean = jnp.mean(mixed_rows, axis=1)
    own_dev = jnp.sum((mixed_rows - own_mean[:, None]) ** 2, axis=1)
    own_count = jnp.full((), width, jnp.float32)
    total, row_average, dev = joined_all((own_count, own_mean, own_dev), "tp", chan_merge)
    inverse_deviation = 1.0 / jnp.sqrt(dev[:, None] / total + 1e-05)
    centered_rows = (mixed_rows - row_average[:, None]) * inverse_deviation
    block_result = (centered_rows * output_norm_gain).astype(jnp.bfloat16)
    scaled_rows = out_grad.astype(jnp.float32) * output_norm_gain
    entire_scaled_rows, entire_normalized_rows = tuple(
        (
            part.astype(jnp.float32)
            for part in turned_gather(
                (scaled_rows.astype(jnp.bfloat16), centered_rows.astype(jnp.bfloat16)), "tp", (1, 1)
            )
        )
    )
    first_moment = jnp.mean(entire_scaled_rows, axis=1, keepdims=True)
    second_moment = jnp.mean(entire_scaled_rows * entire_normalized_rows, axis=1, keepdims=True)
    mixed_gradient = (
        (entire_scaled_rows - first_moment - entire_normalized_rows * second_moment)
        * inverse_deviation
    ).astype(jnp.bfloat16)
    group_mlp = mlp_width // tp_count
    mlp_grad = mixed_gradient.reshape(group_rows, tp_count, -1)[:, :, :group_mlp].reshape(
        group_rows, -1
    )
    grad_down = summed_on_arrival(
        jnp.einsum("rh,rc->hc", hidden, mlp_grad, preferred_element_type=jnp.float32).astype(
            jnp.bfloat16
        ),
        "dp",
        0,
    )
    return (block_result, grad_down)


def solution(mesh):
    return jax.shard_map(
        on_device,
        mesh=mesh,
        in_specs=(
            P(("dp", "tp"), None, None),
            P(),
            P(),
            P(None, "tp"),
            P("tp", None),
            P("tp"),
            P("dp", "tp"),
        ),
        out_specs=(P("dp", "tp"), P(("tp", "dp"), None)),
        check_vma=False,
    )
```

profile of v0, /device:TPU:8, one launch (start us, length us, event | category | flops | bytes accessed | tf_op | source)
XLA Modules:
  0.0 184.7 jit_solution(13328559922858504637)
XLA Ops:
  7.2 0.0 all-gather.3.cloned.1.call-start
  7.2 1.6 copy-done
  8.8 1.8 fusion.26
  10.7 0.4 multiply_reduce_fusion
  11.1 0.2 copy.26
  11.3 0.8 divide_convert_fusion
  12.1 0.7 fusion.6
  12.9 0.1 convert_element_type.74
  13.0 0.8 reshape.145
  13.8 10.4 %all-to-all-start.1 = ((bf16[16,2,576]{2,1,0:T(2,128)(2,1)}), bf16[16,2,576]{2,1,0:T(2,128)(2,1)S(1)}, u32[]{:S(2)}, u32[]{:S(2)}) async-start(bf16[16,2,576]{2,1,0:T(2,128)(2,1)} %reshape.145), calls=%async_computation.1 | async-start | bytes 81920 | tf_op jit(solution)/shard_map/all_to_all | solution.py:103
  24.2 37.1 %all-gather.3.cloned.1.call-done = bf16[384,4096]{1,0:T(8,128)(2,1)} async-done(((bf16[24,4096]{1,0:T(8,128)(2,1)}), bf16[384,4096]{1,0:T(8,128)(2,1)}) %all-gather.3.cloned.1.call-update) | async-done | bytes 3145744 | tf_op jit(solution)/shard_map/all_gather | solution.py:90
  61.3 3.6 %fusion.29 = f32[384,256]{1,0:T(8,128)S(1)} fusion(bf16[384,4096]{1,0:T(8,128)(2,1)} %all-gather.3.cloned.1.call-done, bf16[4096,256]{1,0:T(8,128)(2,1)} %param.10), kind=kOutput, calls=%fused_computation.71 | convolution fusion | flops 805306368 | bytes 5636096 | tf_op jit(solution)/shard_map/dot_general | solution.py:89
  64.9 0.7 copy-done.7
  65.7 0.4 convolution_convert_fusion
  66.1 1.0 copy.19
  67.1 4.3 %all-to-all-start = ((bf16[16,384,48]{1,2,0:T(8,128)(2,1)}), bf16[16,384,48]{1,2,0:T(8,128)(2,1)S(1)}, u32[]{:S(2)}, u32[]{:S(2)}) async-start(bf16[16,384,48]{1,2,0:T(8,128)(2,1)} %bitcast.2), calls=%async_computation | async-start | bytes 1179648 | tf_op jit(solution)/shard_map/all_to_all | solution.py:14
  71.4 0.0 all-gather.5.cloned.1.call-start
  71.5 0.1 reshape.146
  71.6 0.1 convert_reduce_fusion.4
  71.8 0.1 reduce_sum.108
  71.9 0.1 reduce_sum.110
  72.0 0.1 copy.21
  72.1 16.6 %all-to-all-done = bf16[16,384,48]{1,2,0:T(8,128)(2,1)S(1)} async-done(((bf16[16,384,48]{1,2,0:T(8,128)(2,1)}), bf16[16,384,48]{1,2,0:T(8,128)(2,1)S(1)}, u32[]{:S(2)}, u32[]{:S(2)}) %all-to-all-start) | async-done | bytes 589856 | tf_op jit(solution)/shard_map/all_to_all | solution.py:14
  88.7 0.2 convert_reduce_fusion.1
  89.0 12.5 %all_to_all.25 = f32[16,3,384]{2,1,0:T(4,128)S(1)} all-to-all(f32[16,3,384]{2,1,0:T(4,128)S(1)} %broadcast_in_dim.2), channel_id=1, replica_groups=mesh['dp'=32,'tp'=16] {'tp'}, dimensions={0} | all-to-all | bytes 147456 | tf_op jit(solution)/shard_map/all_to_all | solution.py:20
  101.5 0.1 fusion.24
  101.7 0.1 slice_reduce_fusion
  101.8 0.1 slice.104
  101.9 0.1 slice.105
  102.0 0.1 slice.108
  102.1 0.1 slice.109
  102.2 0.1 slice.112
  102.3 0.1 slice.113
  102.4 0.6 fusion.25
  105.6 0.1 multiply_add_fusion
  105.8 0.1 multiply_add_fusion.2
  106.6 0.1 multiply_add_fusion.4
  106.8 0.7 fusion.16
  107.5 0.7 pad_maximum_fusion.1
  108.2 40.1 %all-gather.5.cloned.1.call-done = bf16[1536,768]{1,0:T(8,128)(2,1)} async-done(((bf16[96,768]{1,0:T(8,128)(2,1)}), bf16[1536,768]{1,0:T(8,128)(2,1)}) %all-gather.5.cloned.1.call-update) | async-done | bytes 2359312 | tf_op jit(solution)/shard_map/all_gather | solution.py:56
  148.3 2.2 %convert_reduce_fusion = (f32[384]{0:T(512)S(1)}, f32[384]{0:T(512)S(1)}) fusion(bf16[1536,768]{1,0:T(8,128)(2,1)} %all-gather.5.cloned.1.call-done), kind=kLoop, calls=%fused_computation.2 | loop fusion | flops 2948352 | bytes 2362368 | tf_op jit(solution)/shard_map/reduce_sum | solution.py:123
  150.6 0.1 copy-done.1
  150.7 0.5 fusion.2
  151.2 0.1 slice.140
  151.3 0.4 copy-done.8
  151.7 0.5 fusion.4
  152.2 25.1 %all_to_all.26 = bf16[32,8,768]{2,1,0:T(8,128)(2,1)S(1)} all-to-all(bf16[32,8,768]{2,1,0:T(8,128)(2,1)S(1)} %fusion.4), channel_id=1, replica_groups=mesh['dp'=32,'tp'=16] {'dp'}, dimensions={0} | all-to-all | bytes 786432 | tf_op jit(solution)/shard_map/all_to_all | solution.py:14
  177.2 0.7 convert_reduce_fusion.3
  (50 shorter events, 0.6 us)
Async XLA Ops:
  7.2 1.7 copy-start
  7.2 5.0 %copy-start.3 = (bf16[256,4]{0,1:T(4,128)(2,1)S(1)}, bf16[256,4]{0,1:T(4,128)(2,1)}, u32[]{:S(2)}) copy-start(bf16[256,4]{0,1:T(4,128)(2,1)} %param.9) | copy-start | bytes 6148
  7.2 54.2 %all-gather.3.cloned.1.call-start = ((), (), s32[]{:S(2)}) async-start(), calls=%async_computation.4 | async-start | bytes 3342336 | tf_op jit(solution)/shard_map/all_gather | solution.py:90
  13.8 53.3 %all-to-all-start.1 = ((bf16[16,2,576]{2,1,0:T(2,128)(2,1)}), bf16[16,2,576]{2,1,0:T(2,128)(2,1)S(1)}, u32[]{:S(2)}, u32[]{:S(2)}) async-start(bf16[16,2,576]{2,1,0:T(2,128)(2,1)} %reshape.145), calls=%async_computation.1 | async-start | bytes 81920 | tf_op jit(solution)/shard_map/all_to_all | solution.py:103
  61.3 4.3 %copy-start.6 = (bf16[256,768]{1,0:T(8,128)(2,1)S(1)}, bf16[256,768]{1,0:T(8,128)(2,1)}, u32[]{:S(2)}) copy-start(bf16[256,768]{1,0:T(8,128)(2,1)} %param.11) | copy-start | bytes 1179652
  64.9 0.7 copy-start.7
  66.0 22.9 %copy-start.4 = (f32[1,384]{1,0:T(1,128)S(1)}, f32[1,384]{1,0:T(1,128)}, u32[]{:S(2)}) copy-start(f32[1,384]{1,0:T(1,128)} %constant.29.clone.1) | copy-start | bytes 4612
  66.1 40.7 %copy-start.2 = (bf16[384,96]{0,1:T(8,128)(2,1)S(1)}, bf16[384,96]{0,1:T(8,128)(2,1)}, u32[]{:S(2)}) copy-start(bf16[384,96]{0,1:T(8,128)(2,1)} %param.13) | copy-start | bytes 221188
  66.1 40.7 %copy-start.5 = (f32[96]{0:T(128)S(1)}, f32[96]{0:T(128)}, u32[]{:S(2)}) copy-start(f32[96]{0:T(128)} %param.12) | copy-start | bytes 1156
  67.1 21.5 %all-to-all-start = ((bf16[16,384,48]{1,2,0:T(8,128)(2,1)}), bf16[16,384,48]{1,2,0:T(8,128)(2,1)S(1)}, u32[]{:S(2)}, u32[]{:S(2)}) async-start(bf16[16,384,48]{1,2,0:T(8,128)(2,1)} %bitcast.2), calls=%async_computation | async-start | bytes 1179648 | tf_op jit(solution)/shard_map/all_to_all | solution.py:14
  71.4 76.9 %all-gather.5.cloned.1.call-start = ((), (), s32[]{:S(2)}) async-start(), calls=%async_computation.5 | async-start | bytes 2506752 | tf_op jit(solution)/shard_map/all_gather | solution.py:56
  148.3 2.4 %copy-start.1 = (bf16[1536,768]{1,0:T(8,128)(2,1)S(1)}, bf16[1536,768]{1,0:T(8,128)(2,1)}, u32[]{:S(2)}) copy-start(bf16[1536,768]{1,0:T(8,128)(2,1)} %all-gather.5.cloned.1.call-done) | copy-start | bytes 7077892
  150.7 1.0 copy-start.8
Sparse Core Ops, SparseCore 0:
  12.3 49.0 all-gather.2
  108.3 39.9 all-gather.4
where the time goes:
time: 185 us
  waiting for transfers between devices  93.8 us (51%)
  blocking collectives  37.6 us (20%)
  between operations  17.6 us (10%)
  starting transfers between devices  14.8 us (8%)
  local copies, waits for them, and re-layouts  7.2 us (4%)
  matrix products  6.93 us (4%)
  other arithmetic  6.77 us (4%)
    all_gather x1, waiting for transfers between devices, turned_gather(): filled, at, done = (lax.all_gather(both, axis, axis=0, tiled=True), 0, [])  40.1 us
    all_gather x1, waiting for transfers between devices, on_device(): lax.all_gather(normed, 'tp', axis=0, tiled=True)  37.1 us
    all_to_all x1, blocking collectives, summed_on_arrival(): lax.all_to_all(parts, axis, split_axis=0, concat_axis=0, tiled=True)  25.1 us
    all_to_all x1, waiting for transfers between devices, summed_on_arrival(): lax.all_to_all(parts, axis, split_axis=0, concat_axis=0, tiled=True)  16.6 us
    all_to_all x1, blocking collectives, sent_to_all(): lax.all_to_all(jnp.broadcast_to(x[None], (devices, *x.shape)), axis, 0, 0...  12.5 us
    all_to_all x1, starting transfers between devices, on_device(): lax.all_to_all(lcb.astype(jnp.bfloat16), 'tp', split_axis=1, concat_axis=...  10.4 us
    all_to_all x1, starting transfers between devices, summed_on_arrival(): lax.all_to_all(parts, axis, split_axis=0, concat_axis=0, tiled=True)  4.3 us
    unnamed x22, local copies, waits for them, and re-layouts  4.06 us
  transfers between devices with their start and end apart: 4, of which 3 were waited for; matrix products, arithmetic and copies ran while one was open for 4% of the time, Pallas kernels for 0%

commit v1 on v0

--- a/solution.py
+++ b/solution.py
@@ -2,6 +2,27 @@
 import jax.numpy as jnp
 from jax import lax
 from jax.sharding import PartitionSpec as P
+
+
+def collect(value, axis, dim):
+    size, index, span = (lax.axis_size(axis), lax.axis_index(axis), value.shape[dim])
+    forward = [(i, (i + 1) % size) for i in range(size)]
+    left = [(i, (i - 1) % size) for i in range(size)]
+    out = jnp.zeros((*value.shape[:dim], size * span, *value.shape[dim + 1 :]), value.dtype)
+    out = lax.dynamic_update_slice_in_dim(out, value, index * span, axis=dim)
+    from_left = from_right = value
+    halfway = size // 2
+    for step in range(1, halfway + 1):
+        from_left = lax.ppermute(from_left, axis, forward)
+        out = lax.dynamic_update_slice_in_dim(
+            out, from_left, (index - step) % size * span, axis=dim
+        )
+        if step < size - halfway:
+            from_right = lax.ppermute(from_right, axis, left)
+            out = lax.dynamic_update_slice_in_dim(
+                out, from_right, (index + step) % size * span, axis=dim
+            )
+    return out
 
 
 def split_up(x, dim, devices):
@@ -86,11 +107,7 @@
         "sef,fj->sje", embeddings, compress, preferred_element_type=jnp.float32
     ).reshape(samples, -1)
     hidden = jax.nn.gelu(
-        jnp.dot(
-            lax.all_gather(normed, "tp", axis=0, tiled=True),
-            w_up,
-            preferred_element_type=jnp.float32,
-        ),
+        jnp.dot(collect(normed, "tp", 0), w_up, preferred_element_type=jnp.float32),
         approximate=True,
     ).astype(jnp.bfloat16)
     group_rows = hidden.shape[0]

time: 185 us -> 200 us (1.081)
  starting transfers between devices: 14.8 us -> 37.5 us
  waiting for transfers between devices: 93.8 us -> 74.4 us
  local copies, waits for them, and re-layouts: 7.2 us -> 19.2 us
    all_gather x1 -> x0, waiting for transfers between devices: 37.1 us -> none  [on_device(): lax.all_gather(normed, 'tp', axis=0, tiled=True)]
    ppermute x0 -> x15, starting transfers between devices: none -> 26.2 us  [the longest x7 26.1 us: collect(): from_right = lax.ppermute(from_right, axis, left)]
    ppermute x0 -> x15, waiting for transfers between devices: none -> 17.4 us  [the longest x8 17.3 us: collect(): from_left = lax.ppermute(from_left, axis, forward)]
    dynamic_update_slice x0 -> x15, local copies, waits for them, and re-layouts: none -> 10.3 us  [the longest x8 5.5 us: collect(): lax.dynamic_update_slice_in_dim(out, from_left, (index - step) % size * s...]
    all_to_all x1, starting transfers between devices: 10.4 us -> 4.85 us  [on_device(): lax.all_to_all(lcb.astype(jnp.bfloat16), 'tp', split_axis=1, concat_axis=...]
    all_to_all x1, starting transfers between devices: 4.3 us -> 6.34 us  [summed_on_arrival(): lax.all_to_all(parts, axis, split_axis=0, concat_axis=0, tiled=True)]
    broadcast_in_dim x0 -> x1, local copies, waits for them, and re-layouts: none -> 2 us  [collect(): jnp.zeros((*value.shape[:dim], size * span, *value.shape[dim + 1:]), valu...]
    unnamed x22 -> x24, local copies, waits for them, and re-layouts: 4.06 us -> 3.72 us
  transfers between devices with their start and end apart: 4 -> 18, of which waited for: 3 -> 9; matrix products, arithmetic and copies ran while one was open for 4% -> 8% of each run, Pallas kernels for 0% -> 0%
where the time goes in v1:
time: 200 us
  waiting for transfers between devices  74.4 us (37%)
  blocking collectives  37.6 us (19%)
  starting transfers between devices  37.5 us (19%)
  local copies, waits for them, and re-layouts  19.2 us (10%)
  between operations  17.9 us (9%)
  other arithmetic  6.76 us (3%)
  matrix products  6.3 us (3%)
    all_gather x1, waiting for transfers between devices, turned_gather(): filled, at, done = (lax.all_gather(both, axis, axis=0, tiled=True), 0, [])  40.4 us
    ppermute x7, starting transfers between devices, collect(): from_right = lax.ppermute(from_right, axis, left)  26.1 us
    all_to_all x1, blocking collectives, summed_on_arrival(): lax.all_to_all(parts, axis, split_axis=0, concat_axis=0, tiled=True)  25.1 us
    ppermute x8, waiting for transfers between devices, collect(): from_left = lax.ppermute(from_left, axis, forward)  17.3 us
    all_to_all x1, waiting for transfers between devices, summed_on_arrival(): lax.all_to_all(parts, axis, split_axis=0, concat_axis=0, tiled=True)  16.6 us
    all_to_all x1, blocking collectives, sent_to_all(): lax.all_to_all(jnp.broadcast_to(x[None], (devices, *x.shape)), axis, 0, 0...  12.5 us
    all_to_all x1, starting transfers between devices, summed_on_arrival(): lax.all_to_all(parts, axis, split_axis=0, concat_axis=0, tiled=True)  6.34 us
    dynamic_update_slice x8, local copies, waits for them, and re-layouts, collect(): lax.dynamic_update_slice_in_dim(out, from_left, (index - step) % size * s...  5.5 us
  transfers between devices with their start and end apart: 18, of which 9 were waited for; matrix products, arithmetic and copies ran while one was open for 8% of the time, Pallas kernels for 0%

profile of v1, /device:TPU:8, one launch (start us, length us, event | category | flops | bytes accessed | tf_op | source)
XLA Modules:
  0.0 199.6 jit_solution(2537374468786052102)
XLA Ops:
  7.2 1.7 copy-done
  8.8 1.8 fusion.26
  11.3 2.0 %broadcast_in_dim.4 = bf16[384,4096]{1,0:T(8,128)(2,1)} broadcast(bf16[]{:T(256)} %constant.109.clone.1), dimensions={} | broadcast | bytes 3145730 | tf_op jit(solution)/shard_map/broadcast_in_dim | solution.py:11
  13.3 0.8 constant_dynamic-update-slice_fusion.15
  14.1 8.5 %collective-permute-start.1 = (bf16[24,4096]{1,0:T(8,128)(2,1)S(1)}, bf16[24,4096]{1,0:T(8,128)(2,1)S(1)}, u32[]{:S(2)}, u32[]{:S(2)}) collective-permute-start(bf16[24,4096]{1,0:T(8,128)(2,1)S(1)} %get-tuple-element.19), channel_id=1, source_target_pairs={{0,15},{1,0},{2,1},{3,2},{4,3},{5,4},{6,5},{7,6},{8,7},{9,8},{10,9... | collective-permute-start | bytes 589832 | tf_op jit(solution)/shard_map/ppermute | solution.py:21
  22.6 0.7 fusion.6
  23.5 0.8 reshape.145
  24.3 4.8 %all-to-all-start.1 = ((bf16[16,2,576]{2,1,0:T(2,128)(2,1)}), bf16[16,2,576]{2,1,0:T(2,128)(2,1)S(1)}, u32[]{:S(2)}, u32[]{:S(2)}) async-start(bf16[16,2,576]{2,1,0:T(2,128)(2,1)} %reshape.145), calls=%async_computation.1 | async-start | bytes 81920 | tf_op jit(solution)/shard_map/all_to_all | solution.py:120
  29.6 2.8 %collective-permute-start.3 = (bf16[24,4096]{1,0:T(8,128)(2,1)S(1)}, bf16[24,4096]{1,0:T(8,128)(2,1)S(1)}, u32[]{:S(2)}, u32[]{:S(2)}) collective-permute-start(bf16[24,4096]{1,0:T(8,128)(2,1)S(1)} %collective-permute-done.1), channel_id=1, source_target_pairs={{0,15},{1,0},{2,1},{3,2},{4,3},{5,4},{6,5},{7,6},{8,7},{9,8},{10,9... | collective-permute-start | bytes 589832 | tf_op jit(solution)/shard_map/ppermute | solution.py:21
  32.4 0.7 constant_dynamic-update-slice_fusion.14
  33.1 0.7 constant_dynamic-update-slice_fusion.13
  33.8 2.6 %collective-permute-done.2 = bf16[24,4096]{1,0:T(8,128)(2,1)S(1)} collective-permute-done((bf16[24,4096]{1,0:T(8,128)(2,1)S(1)}, bf16[24,4096]{1,0:T(8,128)(2,1)S(1)}, u32[]{:S(2)}, u32[]{:S(2)}) %collective-permute-start.2) | collective-permute-done | bytes 196640 | tf_op jit(solution)/shard_map/ppermute | solution.py:16
  36.3 3.0 %collective-permute-start.5 = (bf16[24,4096]{1,0:T(8,128)(2,1)S(1)}, bf16[24,4096]{1,0:T(8,128)(2,1)S(1)}, u32[]{:S(2)}, u32[]{:S(2)}) collective-permute-start(bf16[24,4096]{1,0:T(8,128)(2,1)S(1)} %collective-permute-done.3), channel_id=1, source_target_pairs={{0,15},{1,0},{2,1},{3,2},{4,3},{5,4},{6,5},{7,6},{8,7},{9,8},{10,9... | collective-permute-start | bytes 589832 | tf_op jit(solution)/shard_map/ppermute | solution.py:21
  39.3 0.7 constant_dynamic-update-slice_fusion.12
  40.0 0.7 constant_dynamic-update-slice_fusion.11
  40.7 2.0 collective-permute-done.4
  42.7 3.0 %collective-permute-start.7 = (bf16[24,4096]{1,0:T(8,128)(2,1)S(1)}, bf16[24,4096]{1,0:T(8,128)(2,1)S(1)}, u32[]{:S(2)}, u32[]{:S(2)}) collective-permute-start(bf16[24,4096]{1,0:T(8,128)(2,1)S(1)} %collective-permute-done.5), channel_id=1, source_target_pairs={{0,15},{1,0},{2,1},{3,2},{4,3},{5,4},{6,5},{7,6},{8,7},{9,8},{10,9... | collective-permute-start | bytes 589832 | tf_op jit(solution)/shard_map/ppermute | solution.py:21
  45.6 0.7 constant_dynamic-update-slice_fusion.10
  46.3 0.7 constant_dynamic-update-slice_fusion.9
  47.0 2.0 collective-permute-done.6
  49.0 3.0 %collective-permute-start.9 = (bf16[24,4096]{1,0:T(8,128)(2,1)S(1)}, bf16[24,4096]{1,0:T(8,128)(2,1)S(1)}, u32[]{:S(2)}, u32[]{:S(2)}) collective-permute-start(bf16[24,4096]{1,0:T(8,128)(2,1)S(1)} %collective-permute-done.7), channel_id=1, source_target_pairs={{0,15},{1,0},{2,1},{3,2},{4,3},{5,4},{6,5},{7,6},{8,7},{9,8},{10,9... | collective-permute-start | bytes 589832 | tf_op jit(solution)/shard_map/ppermute | solution.py:21
  51.9 0.7 constant_dynamic-update-slice_fusion.8
  52.6 0.7 constant_dynamic-update-slice_fusion.7
  53.3 2.0 collective-permute-done.8
  55.3 3.0 %collective-permute-start.11 = (bf16[24,4096]{1,0:T(8,128)(2,1)S(1)}, bf16[24,4096]{1,0:T(8,128)(2,1)S(1)}, u32[]{:S(2)}, u32[]{:S(2)}) collective-permute-start(bf16[24,4096]{1,0:T(8,128)(2,1)S(1)} %collective-permute-done.9), channel_id=1, source_target_pairs={{0,15},{1,0},{2,1},{3,2},{4,3},{5,4},{6,5},{7,6},{8,7},{9,8},{10,9... | collective-permute-start | bytes 589832 | tf_op jit(solution)/shard_map/ppermute | solution.py:21
  58.2 0.7 constant_dynamic-update-slice_fusion.6
  58.9 0.7 constant_dynamic-update-slice_fusion.5
  59.6 2.0 collective-permute-done.10
  61.6 3.0 %collective-permute-start.13 = (bf16[24,4096]{1,0:T(8,128)(2,1)S(1)}, bf16[24,4096]{1,0:T(8,128)(2,1)S(1)}, u32[]{:S(2)}, u32[]{:S(2)}) collective-permute-start(bf16[24,4096]{1,0:T(8,128)(2,1)S(1)} %collective-permute-done.11), channel_id=1, source_target_pairs={{0,15},{1,0},{2,1},{3,2},{4,3},{5,4},{6,5},{7,6},{8,7},{9,8},{10,9... | collective-permute-start | bytes 589832 | tf_op jit(solution)/shard_map/ppermute | solution.py:21
  64.5 0.7 constant_dynamic-update-slice_fusion.4
  65.2 0.7 constant_dynamic-update-slice_fusion.3
  65.9 1.9 collective-permute-done.12
  67.9 0.7 constant_dynamic-update-slice_fusion.2
  68.6 0.7 constant_dynamic-update-slice_fusion.1
  69.2 4.9 %collective-permute-done.14 = bf16[24,4096]{1,0:T(8,128)(2,1)S(1)} collective-permute-done((bf16[24,4096]{1,0:T(8,128)(2,1)S(1)}, bf16[24,4096]{1,0:T(8,128)(2,1)S(1)}, u32[]{:S(2)}, u32[]{:S(2)}) %collective-permute-start.14) | collective-permute-done | bytes 196640 | tf_op jit(solution)/shard_map/ppermute | solution.py:16
  74.2 0.7 constant_dynamic-update-slice_fusion
  74.9 2.9 %fusion.29 = f32[384,256]{1,0:T(8,128)S(1)} fusion(bf16[384,4096]{1,0:T(8,128)(2,1)} %constant_dynamic-update-slice_fusion, bf16[4096,256]{1,0:T(8,128)(2,1)S(1)} %copy-done.6), kind=kOutput, calls=%fused_computation.87 | convolution fusion | flops 805306368 | bytes 5636096 | tf_op jit(solution)/shard_map/dot_general | solution.py:110
  77.8 0.7 copy-done.8
  78.9 1.0 copy.19
  80.0 6.3 %all-to-all-start = ((bf16[16,384,48]{1,2,0:T(8,128)(2,1)}), bf16[16,384,48]{1,2,0:T(8,128)(2,1)S(1)}, u32[]{:S(2)}, u32[]{:S(2)}) async-start(bf16[16,384,48]{1,2,0:T(8,128)(2,1)} %bitcast.2), calls=%async_computation | async-start | bytes 1179648 | tf_op jit(solution)/shard_map/all_to_all | solution.py:35
  87.0 16.6 %all-to-all-done = bf16[16,384,48]{1,2,0:T(8,128)(2,1)S(1)} async-done(((bf16[16,384,48]{1,2,0:T(8,128)(2,1)}), bf16[16,384,48]{1,2,0:T(8,128)(2,1)S(1)}, u32[]{:S(2)}, u32[]{:S(2)}) %all-to-all-start) | async-done | bytes 589856 | tf_op jit(solution)/shard_map/all_to_all | solution.py:35
  103.9 12.5 %all_to_all.25 = f32[16,3,384]{2,1,0:T(4,128)S(1)} all-to-all(f32[16,3,384]{2,1,0:T(4,128)S(1)} %broadcast_in_dim.5), channel_id=1, replica_groups=mesh['dp'=32,'tp'=16] {'tp'}, dimensions={0} | all-to-all | bytes 147456 | tf_op jit(solution)/shard_map/all_to_all | solution.py:41
  121.7 0.7 fusion.16
  122.4 0.7 pad_maximum_fusion.1
  123.1 40.4 %all-gather.2.cloned.1.call-done = bf16[1536,768]{1,0:T(8,128)(2,1)} async-done(((bf16[96,768]{1,0:T(8,128)(2,1)}), bf16[1536,768]{1,0:T(8,128)(2,1)}) %all-gather.2.cloned.1.call-update) | async-done | bytes 2359312 | tf_op jit(solution)/shard_map/all_gather | solution.py:77
  163.5 2.2 %convert_reduce_fusion = (f32[384]{0:T(512)S(1)}, f32[384]{0:T(512)S(1)}) fusion(bf16[1536,768]{1,0:T(8,128)(2,1)} %all-gather.2.cloned.1.call-done), kind=kLoop, calls=%fused_computation.2 | loop fusion | flops 2948352 | bytes 2362368 | tf_op jit(solution)/shard_map/reduce_sum | solution.py:140
  167.0 25.1 %all_to_all.26 = bf16[32,8,768]{2,1,0:T(8,128)(2,1)S(1)} all-to-all(bf16[32,8,768]{2,1,0:T(8,128)(2,1)S(1)} %fusion.4), channel_id=1, replica_groups=mesh['dp'=32,'tp'=16] {'dp'}, dimensions={0} | all-to-all | bytes 786432 | tf_op jit(solution)/shard_map/all_to_all | solution.py:35
  192.1 0.7 convert_reduce_fusion.3
  (95 shorter events, 5.4 us)
Async XLA Ops:
  7.2 1.7 copy-start
  10.7 11.9 %copy-start.3 = (bf16[256,4]{0,1:T(4,128)(2,1)S(1)}, bf16[256,4]{0,1:T(4,128)(2,1)}, u32[]{:S(2)}) copy-start(bf16[256,4]{0,1:T(4,128)(2,1)} %param.9) | copy-start | bytes 6148
  14.1 15.3 %collective-permute-start = (bf16[24,4096]{1,0:T(8,128)(2,1)S(1)}, bf16[24,4096]{1,0:T(8,128)(2,1)S(1)}, u32[]{:S(2)}, u32[]{:S(2)}) collective-permute-start(bf16[24,4096]{1,0:T(8,128)(2,1)S(1)} %get-tuple-element.19), channel_id=1, source_target_pairs={{0,1},{1,2},{2,3},{3,4},{4,5},{5,6},{6,7},{7,8},{8,9},{9,10},{10,1... | collective-permute-start | bytes 589832 | tf_op jit(solution)/shard_map/ppermute | solution.py:16
  14.1 15.4 %collective-permute-start.1 = (bf16[24,4096]{1,0:T(8,128)(2,1)S(1)}, bf16[24,4096]{1,0:T(8,128)(2,1)S(1)}, u32[]{:S(2)}, u32[]{:S(2)}) collective-permute-start(bf16[24,4096]{1,0:T(8,128)(2,1)S(1)} %get-tuple-element.19), channel_id=1, source_target_pairs={{0,15},{1,0},{2,1},{3,2},{4,3},{5,4},{6,5},{7,6},{8,7},{9,8},{10,9... | collective-permute-start | bytes 589832 | tf_op jit(solution)/shard_map/ppermute | solution.py:21
  24.3 55.7 %all-to-all-start.1 = ((bf16[16,2,576]{2,1,0:T(2,128)(2,1)}), bf16[16,2,576]{2,1,0:T(2,128)(2,1)S(1)}, u32[]{:S(2)}, u32[]{:S(2)}) async-start(bf16[16,2,576]{2,1,0:T(2,128)(2,1)} %reshape.145), calls=%async_computation.1 | async-start | bytes 81920 | tf_op jit(solution)/shard_map/all_to_all | solution.py:120
  29.4 45.5 %copy-start.6 = (bf16[4096,256]{1,0:T(8,128)(2,1)S(1)}, bf16[4096,256]{1,0:T(8,128)(2,1)}, u32[]{:S(2)}) copy-start(bf16[4096,256]{1,0:T(8,128)(2,1)} %param.10) | copy-start | bytes 6291460
  29.4 6.9 %collective-permute-start.2 = (bf16[24,4096]{1,0:T(8,128)(2,1)S(1)}, bf16[24,4096]{1,0:T(8,128)(2,1)S(1)}, u32[]{:S(2)}, u32[]{:S(2)}) collective-permute-start(bf16[24,4096]{1,0:T(8,128)(2,1)S(1)} %collective-permute-done), channel_id=1, source_target_pairs={{0,1},{1,2},{2,3},{3,4},{4,5},{5,6},{6,7},{7,8},{8,9},{9,10},{10,1... | collective-permute-start | bytes 589832 | tf_op jit(solution)/shard_map/ppermute | solution.py:16
  29.6 6.8 %collective-permute-start.3 = (bf16[24,4096]{1,0:T(8,128)(2,1)S(1)}, bf16[24,4096]{1,0:T(8,128)(2,1)S(1)}, u32[]{:S(2)}, u32[]{:S(2)}) collective-permute-start(bf16[24,4096]{1,0:T(8,128)(2,1)S(1)} %collective-permute-done.1), channel_id=1, source_target_pairs={{0,15},{1,0},{2,1},{3,2},{4,3},{5,4},{6,5},{7,6},{8,7},{9,8},{10,9... | collective-permute-start | bytes 589832 | tf_op jit(solution)/shard_map/ppermute | solution.py:21
  36.3 6.3 %collective-permute-start.4 = (bf16[24,4096]{1,0:T(8,128)(2,1)S(1)}, bf16[24,4096]{1,0:T(8,128)(2,1)S(1)}, u32[]{:S(2)}, u32[]{:S(2)}) collective-permute-start(bf16[24,4096]{1,0:T(8,128)(2,1)S(1)} %collective-permute-done.2), channel_id=1, source_target_pairs={{0,1},{1,2},{2,3},{3,4},{4,5},{5,6},{6,7},{7,8},{8,9},{9,10},{10,1... | collective-permute-start | bytes 589832 | tf_op jit(solution)/shard_map/ppermute | solution.py:16
  36.3 6.3 %collective-permute-start.5 = (bf16[24,4096]{1,0:T(8,128)(2,1)S(1)}, bf16[24,4096]{1,0:T(8,128)(2,1)S(1)}, u32[]{:S(2)}, u32[]{:S(2)}) collective-permute-start(bf16[24,4096]{1,0:T(8,128)(2,1)S(1)} %collective-permute-done.3), channel_id=1, source_target_pairs={{0,15},{1,0},{2,1},{3,2},{4,3},{5,4},{6,5},{7,6},{8,7},{9,8},{10,9... | collective-permute-start | bytes 589832 | tf_op jit(solution)/shard_map/ppermute | solution.py:21
  42.6 6.3 %collective-permute-start.6 = (bf16[24,4096]{1,0:T(8,128)(2,1)S(1)}, bf16[24,4096]{1,0:T(8,128)(2,1)S(1)}, u32[]{:S(2)}, u32[]{:S(2)}) collective-permute-start(bf16[24,4096]{1,0:T(8,128)(2,1)S(1)} %collective-permute-done.4), channel_id=1, source_target_pairs={{0,1},{1,2},{2,3},{3,4},{4,5},{5,6},{6,7},{7,8},{8,9},{9,10},{10,1... | collective-permute-start | bytes 589832 | tf_op jit(solution)/shard_map/ppermute | solution.py:16
  42.7 6.3 %collective-permute-start.7 = (bf16[24,4096]{1,0:T(8,128)(2,1)S(1)}, bf16[24,4096]{1,0:T(8,128)(2,1)S(1)}, u32[]{:S(2)}, u32[]{:S(2)}) collective-permute-start(bf16[24,4096]{1,0:T(8,128)(2,1)S(1)} %collective-permute-done.5), channel_id=1, source_target_pairs={{0,15},{1,0},{2,1},{3,2},{4,3},{5,4},{6,5},{7,6},{8,7},{9,8},{10,9... | collective-permute-start | bytes 589832 | tf_op jit(solution)/shard_map/ppermute | solution.py:21
  49.0 6.3 %collective-permute-start.8 = (bf16[24,4096]{1,0:T(8,128)(2,1)S(1)}, bf16[24,4096]{1,0:T(8,128)(2,1)S(1)}, u32[]{:S(2)}, u32[]{:S(2)}) collective-permute-start(bf16[24,4096]{1,0:T(8,128)(2,1)S(1)} %collective-permute-done.6), channel_id=1, source_target_pairs={{0,1},{1,2},{2,3},{3,4},{4,5},{5,6},{6,7},{7,8},{8,9},{9,10},{10,1... | collective-permute-start | bytes 589832 | tf_op jit(solution)/shard_map/ppermute | solution.py:16
  49.0 6.3 %collective-permute-start.9 = (bf16[24,4096]{1,0:T(8,128)(2,1)S(1)}, bf16[24,4096]{1,0:T(8,128)(2,1)S(1)}, u32[]{:S(2)}, u32[]{:S(2)}) collective-permute-start(bf16[24,4096]{1,0:T(8,128)(2,1)S(1)} %collective-permute-done.7), channel_id=1, source_target_pairs={{0,15},{1,0},{2,1},{3,2},{4,3},{5,4},{6,5},{7,6},{8,7},{9,8},{10,9... | collective-permute-start | bytes 589832 | tf_op jit(solution)/shard_map/ppermute | solution.py:21
  55.3 6.3 %collective-permute-start.10 = (bf16[24,4096]{1,0:T(8,128)(2,1)S(1)}, bf16[24,4096]{1,0:T(8,128)(2,1)S(1)}, u32[]{:S(2)}, u32[]{:S(2)}) collective-permute-start(bf16[24,4096]{1,0:T(8,128)(2,1)S(1)} %collective-permute-done.8), channel_id=1, source_target_pairs={{0,1},{1,2},{2,3},{3,4},{4,5},{5,6},{6,7},{7,8},{8,9},{9,10},{10,1... | collective-permute-start | bytes 589832 | tf_op jit(solution)/shard_map/ppermute | solution.py:16
  55.3 6.3 %collective-permute-start.11 = (bf16[24,4096]{1,0:T(8,128)(2,1)S(1)}, bf16[24,4096]{1,0:T(8,128)(2,1)S(1)}, u32[]{:S(2)}, u32[]{:S(2)}) collective-permute-start(bf16[24,4096]{1,0:T(8,128)(2,1)S(1)} %collective-permute-done.9), channel_id=1, source_target_pairs={{0,15},{1,0},{2,1},{3,2},{4,3},{5,4},{6,5},{7,6},{8,7},{9,8},{10,9... | collective-permute-start | bytes 589832 | tf_op jit(solution)/shard_map/ppermute | solution.py:21
  61.6 6.3 %collective-permute-start.12 = (bf16[24,4096]{1,0:T(8,128)(2,1)S(1)}, bf16[24,4096]{1,0:T(8,128)(2,1)S(1)}, u32[]{:S(2)}, u32[]{:S(2)}) collective-permute-start(bf16[24,4096]{1,0:T(8,128)(2,1)S(1)} %collective-permute-done.10), channel_id=1, source_target_pairs={{0,1},{1,2},{2,3},{3,4},{4,5},{5,6},{6,7},{7,8},{8,9},{9,10},{10,1... | collective-permute-start | bytes 589832 | tf_op jit(solution)/shard_map/ppermute | solution.py:16
  61.6 7.0 %collective-permute-start.13 = (bf16[24,4096]{1,0:T(8,128)(2,1)S(1)}, bf16[24,4096]{1,0:T(8,128)(2,1)S(1)}, u32[]{:S(2)}, u32[]{:S(2)}) collective-permute-start(bf16[24,4096]{1,0:T(8,128)(2,1)S(1)} %collective-permute-done.11), channel_id=1, source_target_pairs={{0,15},{1,0},{2,1},{3,2},{4,3},{5,4},{6,5},{7,6},{8,7},{9,8},{10,9... | collective-permute-start | bytes 589832 | tf_op jit(solution)/shard_map/ppermute | solution.py:21
  67.9 6.3 %collective-permute-start.14 = (bf16[24,4096]{1,0:T(8,128)(2,1)S(1)}, bf16[24,4096]{1,0:T(8,128)(2,1)S(1)}, u32[]{:S(2)}, u32[]{:S(2)}) collective-permute-start(bf16[24,4096]{1,0:T(8,128)(2,1)S(1)} %collective-permute-done.12), channel_id=1, source_target_pairs={{0,1},{1,2},{2,3},{3,4},{4,5},{5,6},{6,7},{7,8},{8,9},{9,10},{10,1... | collective-permute-start | bytes 589832 | tf_op jit(solution)/shard_map/ppermute | solution.py:16
  74.9 3.7 %copy-start.7 = (bf16[256,768]{1,0:T(8,128)(2,1)S(1)}, bf16[256,768]{1,0:T(8,128)(2,1)}, u32[]{:S(2)}) copy-start(bf16[256,768]{1,0:T(8,128)(2,1)} %param.11) | copy-start | bytes 1179652
  77.8 0.7 copy-start.8
  78.5 25.3 %copy-start.4 = (f32[1,384]{1,0:T(1,128)S(1)}, f32[1,384]{1,0:T(1,128)}, u32[]{:S(2)}) copy-start(f32[1,384]{1,0:T(1,128)} %constant.139.clone.1) | copy-start | bytes 4612
  78.5 43.1 %copy-start.2 = (bf16[384,96]{0,1:T(8,128)(2,1)S(1)}, bf16[384,96]{0,1:T(8,128)(2,1)}, u32[]{:S(2)}) copy-start(bf16[384,96]{0,1:T(8,128)(2,1)} %param.13) | copy-start | bytes 221188
  78.5 43.1 %copy-start.5 = (f32[96]{0:T(128)S(1)}, f32[96]{0:T(128)}, u32[]{:S(2)}) copy-start(f32[96]{0:T(128)} %param.12) | copy-start | bytes 1156
  80.0 23.6 %all-to-all-start = ((bf16[16,384,48]{1,2,0:T(8,128)(2,1)}), bf16[16,384,48]{1,2,0:T(8,128)(2,1)S(1)}, u32[]{:S(2)}, u32[]{:S(2)}) async-start(bf16[16,384,48]{1,2,0:T(8,128)(2,1)} %bitcast.2), calls=%async_computation | async-start | bytes 1179648 | tf_op jit(solution)/shard_map/all_to_all | solution.py:35
  86.3 77.2 %all-gather.2.cloned.1.call-start = ((), (), s32[]{:S(2)}) async-start(), calls=%async_computation.4 | async-start | bytes 2506752 | tf_op jit(solution)/shard_map/all_gather | solution.py:77
  163.5 2.4 %copy-start.1 = (bf16[1536,768]{1,0:T(8,128)(2,1)S(1)}, bf16[1536,768]{1,0:T(8,128)(2,1)}, u32[]{:S(2)}) copy-start(bf16[1536,768]{1,0:T(8,128)(2,1)} %all-gather.2.cloned.1.call-done) | copy-start | bytes 7077892
  163.5 3.0 %copy-start.9 = (f32[384,256]{1,0:T(8,128)S(1)}, f32[384,256]{1,0:T(8,128)}, u32[]{:S(2)}) copy-start(f32[384,256]{1,0:T(8,128)} %copy-done.8) | copy-start | bytes 1179652
Sparse Core Ops, SparseCore 0:
  123.2 40.2 all-gather.1
